TPU v7x, 512 devices: a whole 4x8x8 slice. The times are simulated.
512 devices in a mesh: freq: 16 (over y, core), bl: 32 (over z, x).
Axes of the slice: x: 4, y: 8, z: 8, core: 2. Of those that a mesh axis runs over, the one named last changes fastest.
Arguments:
- visibilities: bfloat16 [2, 64, 2, 32768], P(None, 'freq', None, 'bl'), may hold values from -168 to 168
- predicted_sky: bfloat16 [6, 2, 64, 2, 32768], P(None, None, 'freq', None, 'bl'), may hold values from -2 to 2
- station_pairs: int32 [2, 32768], P(None, 'bl'), may hold values from 0 to 511, as said below
- start_gains: float32 [2, 6, 64, 512], P(None, None, 'freq'), may hold values from 0.1 to 1.9
- kernel_width: int32 [6], replicated, may hold values from 1 to 2
Outputs:
- gains: float32 [2, 6, 64, 512], P(None, None, 'freq')
Inputs may be any that keep to these rules, and one draw needn't show every extreme that they name: `station_pairs`: the two stations of a baseline differ; every station is the first station of some baselines.
All inputs are finite; a program needn't handle non-finite values.
Results may differ from a plain program's by a relative error of at most 0.0003.
Values sent between devices are 32-bit elements; how exact they have to be, the bound alone decides.
A program may use at most 64 MiB of HBM per device.

v0:
```python
import jax
import jax.numpy as jnp
from jax import lax
from jax.sharding import PartitionSpec as P

ITERS = 4


def padded_2(x, sides, width):
    for axis, dim in sides:
        count, length = (lax.axis_size(axis), x.shape[dim])
        up = [(i, (i + 1) % count) for i in range(count - 1)]
        down = [(j, i) for i, j in up]
        last = lax.slice_in_dim(x, length - width, length, axis=dim)
        initial = lax.slice_in_dim(x, 0, width, axis=dim)
        before = lax.ppermute(last, axis, up)
        after = lax.ppermute(initial, axis, down)
        x = jnp.concatenate([before, x, after], axis=dim)
    return x


def station_terms(left_re, left_im, right_re, right_im, sky_re, sky_im, vis_re, vis_im, time_axis):
    fwd_re = left_re * sky_re - left_im * sky_im
    fwd_im = left_re * sky_im + left_im * sky_re
    bwd_re = right_re * sky_re + right_im * sky_im
    bwd_im = right_re * sky_im - right_im * sky_re
    one_re = fwd_re * right_re + fwd_im * right_im
    one_im = fwd_im * right_re - fwd_re * right_im
    res_re = vis_re - jnp.sum(one_re, axis=0) + one_re
    res_im = vis_im - jnp.sum(one_im, axis=0) + one_im
    first_stop_index = jnp.stack(
        [
            jnp.sum(res_re * bwd_re + res_im * bwd_im, axis=time_axis),
            jnp.sum(res_im * bwd_re - res_re * bwd_im, axis=time_axis),
            jnp.sum(bwd_re * bwd_re + bwd_im * bwd_im, axis=time_axis),
        ]
    )
    trailing_stop_index = jnp.stack(
        [
            jnp.sum(res_re * fwd_re + res_im * fwd_im, axis=time_axis),
            jnp.sum(res_re * fwd_im - res_im * fwd_re, axis=time_axis),
            jnp.sum(fwd_re * fwd_re + fwd_im * fwd_im, axis=time_axis),
        ]
    )
    return (first_stop_index.astype(jnp.bfloat16), trailing_stop_index.astype(jnp.bfloat16))


def local_normals(
    gain_now, visibilities, predicted_sky, leading_station, second_station, station_ids
):
    directions = gain_now.shape[1]
    chans = gain_now.shape[2]
    stations = gain_now.shape[3]
    blocal = leading_station.shape[0]
    left_gain = jnp.take(gain_now, leading_station, axis=3)[:, :, :, None, :]
    right_gain = jnp.take(gain_now, second_station, axis=3)[:, :, :, None, :]
    first_stop_index, trailing_stop_index = station_terms(
        left_gain[0],
        left_gain[1],
        right_gain[0],
        right_gain[1],
        predicted_sky[:, 0],
        predicted_sky[:, 1],
        visibilities[0],
        visibilities[1],
        2,
    )
    stacked = jnp.concatenate([first_stop_index, trailing_stop_index], axis=3).reshape(
        3 * directions * chans, 2 * blocal
    )
    block_count = max(1, 2 * blocal // 2048)
    block_size = 2 * blocal // block_count

    def add_block(block_num, running):
        one_hot = (
            station_ids[:, None] == lax.broadcasted_iota(jnp.int32, (block_size, stations), 1)
        ).astype(jnp.bfloat16)
        return running + jnp.dot(stacked, one_hot, preferred_element_type=jnp.float32)

    running = jnp.zeros((3 * directions * chans, stations), jnp.float32)
    running = lax.fori_loop(0, block_count, add_block, running)
    return running.reshape(3, directions, chans, stations)


def update_gains(normals, current, regular_weight):
    solved = (normals[0:2] + regular_weight * current) / (normals[2][None] + regular_weight)
    return 0.5 * (current + solved)


def smooth_gains(padded, weights, totals):
    return (
        jnp.einsum("doj,rdjs->rdos", weights, padded, precision=lax.Precision.HIGHEST)
        / totals[None, :, :, None]
    )


def body(visibilities, predicted_sky, station_pairs, start_gains, kernel_width):
    leading_station = station_pairs[0]
    second_station = station_pairs[1]
    station_ids = jnp.concatenate([leading_station, second_station])
    chans = start_gains.shape[2]
    stations = start_gains.shape[3]
    blocal = station_pairs.shape[1]
    nbl_count = lax.axis_size("bl")
    freq_count = lax.axis_size("freq")
    regular_weight = visibilities.shape[2] * blocal * nbl_count / stations
    base_chan = lax.axis_index("freq") * chans
    out_pos = base_chan + jnp.arange(chans, dtype=jnp.int32)
    in_pos = base_chan - chans + jnp.arange(3 * chans, dtype=jnp.int32)
    gain_shifts = in_pos[None, :] - out_pos[:, None]
    inside = (
        (jnp.abs(gain_shifts) <= chans)
        & (in_pos[None, :] >= 0)
        & (in_pos[None, :] < chans * freq_count)
    )
    spread = kernel_width.astype(jnp.float32)[:, None, None]
    distance = gain_shifts.astype(jnp.float32)[None]
    weights = jnp.where(
        inside[None], jnp.exp(-(distance * distance) / (2.0 * spread * spread)), 0.0
    )
    totals = jnp.sum(weights, axis=2)
    gain_now = start_gains
    for sweep in range(ITERS):
        partial_normals = local_normals(
            gain_now, visibilities, predicted_sky, leading_station, second_station, station_ids
        )
        summed = lax.psum(partial_normals, "bl")
        updated = update_gains(summed, gain_now, regular_weight)
        padded = padded_2(updated, (("freq", 2),), chans)
        gain_now = smooth_gains(padded, weights, totals)
    return gain_now


def solution(mesh):
    in_specs = (
        P(None, "freq", None, "bl"),
        P(None, None, "freq", None, "bl"),
        P(None, "bl"),
        P(None, None, "freq", None),
        P(),
    )
    out_specs = P(None, None, "freq", None)
    return jax.shard_map(body, mesh=mesh, in_specs=in_specs, out_specs=out_specs, check_vma=False)
```

profile of v0, /device:TPU:32, one launch (start us, length us, event | category | flops | bytes accessed | tf_op | source)
XLA Modules:
  0.0 863.9 jit_solution(12639208338049863674)
XLA Ops:
  9.1 10.0 %gather_fusion.1 = f32[1024,2,6,4]{2,3,1,0:T(4,128)} fusion(f32[2,6,4,512]{1,2,3,0:T(4,128)S(1)} %copy.66, s32[1024]{0:T(1024)S(1)} %fusion.144), kind=kCustom, calls=%fused_computation.1.clone | custom fusion | bytes 397312 | tf_op jit(solution)/shard_map/jit(_take)/gather | solution.py:56
  19.1 5.7 select_bitcast_fusion.6
  24.8 2.1 slice_bitcast_fusion.13
  26.8 1.9 copy.71
  29.6 11.7 %gather_fusion = f32[1024,2,6,4]{2,3,1,0:T(4,128)} fusion(f32[2,6,4,512]{1,2,3,0:T(4,128)} %copy-done.1, s32[1024]{0:T(1024)S(1)} %fusion.143), kind=kCustom, calls=%fused_computation.clone | custom fusion | bytes 397312 | tf_op jit(solution)/shard_map/jit(_take)/gather | solution.py:55
  41.3 5.7 select_bitcast_fusion.7
  46.9 2.1 slice_bitcast_fusion.15
  49.0 1.9 copy.67
  52.5 2.1 add_reduce_fusion.15
  56.8 158.0 %all-reduce.5.cloned.1.call-done = f32[3,6,4,512]{3,1,2,0:T(8,128)} async-done(((f32[3,6,4,512]{3,1,2,0:T(8,128)}), f32[3,6,4,512]{3,1,2,0:T(8,128)}) %all-reduce.5.cloned.1.call-update) | async-done | bytes 147472 | tf_op jit(solution)/shard_map/psum | solution.py:127
  216.6 1.9 collective-permute-start.1
  218.6 2.6 collective-permute-start
  221.4 4.6 collective-permute-done
  227.7 10.1 %gather_fusion.3 = f32[1024,2,6,4]{2,3,1,0:T(4,128)} fusion(f32[2,6,4,512]{1,2,3,0:T(4,128)S(1)} %copy.84, s32[1024]{0:T(1024)S(1)} %fusion.144), kind=kCustom, calls=%fused_computation.3.clone | custom fusion | bytes 397312 | tf_op jit(solution)/shard_map/jit(_take)/gather | solution.py:56
  237.7 10.0 %gather_fusion.2 = f32[1024,2,6,4]{2,3,1,0:T(4,128)} fusion(f32[2,6,4,512]{1,2,3,0:T(4,128)S(1)} %copy.84, s32[1024]{0:T(1024)S(1)} %fusion.143), kind=kCustom, calls=%fused_computation.2.clone | custom fusion | bytes 397312 | tf_op jit(solution)/shard_map/jit(_take)/gather | solution.py:55
  247.8 5.7 select_bitcast_fusion.4
  253.4 2.1 slice_bitcast_fusion.9
  255.5 1.9 copy.88
  258.2 5.7 select_bitcast_fusion.5
  263.9 2.1 slice_bitcast_fusion.11
  266.0 1.9 copy.85
  269.4 2.1 add_reduce_fusion.11
  273.5 151.1 %all-reduce.7.cloned.1.call-done = f32[3,6,4,512]{3,1,2,0:T(8,128)} async-done(((f32[3,6,4,512]{3,1,2,0:T(8,128)}), f32[3,6,4,512]{3,1,2,0:T(8,128)}) %all-reduce.7.cloned.1.call-update) | async-done | bytes 147472 | tf_op jit(solution)/shard_map/psum | solution.py:127
  426.4 1.9 collective-permute-start.3
  428.4 2.6 collective-permute-start.2
  431.0 4.9 collective-permute-done.2
  437.5 10.1 %gather_fusion.5 = f32[1024,2,6,4]{2,3,1,0:T(4,128)} fusion(f32[2,6,4,512]{1,2,3,0:T(4,128)S(1)} %copy.98, s32[1024]{0:T(1024)S(1)} %fusion.144), kind=kCustom, calls=%fused_computation.5.clone | custom fusion | bytes 397312 | tf_op jit(solution)/shard_map/jit(_take)/gather | solution.py:56
  447.5 10.0 %gather_fusion.4 = f32[1024,2,6,4]{2,3,1,0:T(4,128)} fusion(f32[2,6,4,512]{1,2,3,0:T(4,128)S(1)} %copy.98, s32[1024]{0:T(1024)S(1)} %fusion.143), kind=kCustom, calls=%fused_computation.4.clone | custom fusion | bytes 397312 | tf_op jit(solution)/shard_map/jit(_take)/gather | solution.py:55
  457.6 5.7 select_bitcast_fusion.2
  463.2 2.1 slice_bitcast_fusion.5
  468.0 5.7 select_bitcast_fusion.3
  473.7 2.1 slice_bitcast_fusion.7
  479.2 2.1 add_reduce_fusion.7
  483.3 151.2 %all-reduce.9.cloned.1.call-done = f32[3,6,4,512]{3,1,2,0:T(8,128)} async-done(((f32[3,6,4,512]{3,1,2,0:T(8,128)}), f32[3,6,4,512]{3,1,2,0:T(8,128)}) %all-reduce.9.cloned.1.call-update) | async-done | bytes 147472 | tf_op jit(solution)/shard_map/psum | solution.py:127
  636.3 1.9 collective-permute-start.5
  638.2 2.7 collective-permute-start.4
  640.9 4.8 collective-permute-done.4
  647.4 10.1 %gather_fusion.7 = f32[1024,2,6,4]{2,3,1,0:T(4,128)} fusion(f32[2,6,4,512]{1,2,3,0:T(4,128)S(1)} %copy.112, s32[1024]{0:T(1024)S(1)} %fusion.144), kind=kCustom, calls=%fused_computation.7.clone | custom fusion | bytes 397312 | tf_op jit(solution)/shard_map/jit(_take)/gather | solution.py:56
  657.4 10.0 %gather_fusion.6 = f32[1024,2,6,4]{2,3,1,0:T(4,128)} fusion(f32[2,6,4,512]{1,2,3,0:T(4,128)S(1)} %copy.112, s32[1024]{0:T(1024)S(1)} %fusion.143), kind=kCustom, calls=%fused_computation.6.clone | custom fusion | bytes 397312 | tf_op jit(solution)/shard_map/jit(_take)/gather | solution.py:55
  667.4 5.7 select_bitcast_fusion
  673.1 2.1 slice_bitcast_fusion.1
  677.9 5.7 select_bitcast_fusion.1
  683.6 2.1 slice_bitcast_fusion.3
  689.1 2.1 add_reduce_fusion.3
  693.1 151.1 %all-reduce.11.cloned.1.call-done = f32[3,6,4,512]{3,1,2,0:T(8,128)} async-done(((f32[3,6,4,512]{3,1,2,0:T(8,128)}), f32[3,6,4,512]{3,1,2,0:T(8,128)}) %all-reduce.11.cloned.1.call-update) | async-done | bytes 147472 | tf_op jit(solution)/shard_map/psum | solution.py:127
  846.1 1.9 collective-permute-start.7
  848.0 2.4 collective-permute-start.6
  850.5 5.0 collective-permute-done.6
  (110 shorter events, 41.3 us)
Async XLA Ops:
  6.5 208.3 %all-reduce.5.cloned.1.call-start = ((), (), s32[]{:S(2)}) async-start(), calls=%async_computation | async-start | bytes 393216 | tf_op jit(solution)/shard_map/psum | solution.py:127
  9.0 10.1 %copy-start.1 = (f32[2,6,4,512]{1,2,3,0:T(4,128)}, f32[2,6,4,512]{1,2,3,0:T(4,128)S(1)}, u32[]{:S(2)}) copy-start(f32[2,6,4,512]{1,2,3,0:T(4,128)S(1)} %copy.66) | copy-start | bytes 294916
  49.0 2.8 copy-start
  49.0 3.4 copy-start.2
  51.8 5.0 copy-start.4
  51.8 163.9 %copy-start.3 = (f32[2,6,4,512]{3,2,1,0:T(4,128)S(1)}, f32[2,6,4,512]{3,2,1,0:T(4,128)}, u32[]{:S(2)}) copy-start(f32[2,6,4,512]{3,2,1,0:T(4,128)} %param.10) | copy-start | bytes 294916
  56.5 368.0 %all-reduce.7.cloned.1.call-start = ((), (), s32[]{:S(2)}) async-start(), calls=%async_computation.1 | async-start | bytes 393216 | tf_op jit(solution)/shard_map/psum | solution.py:127
  216.6 4.8 collective-permute-start.1
  218.6 7.5 collective-permute-start
  273.5 361.0 %all-reduce.9.cloned.1.call-start = ((), (), s32[]{:S(2)}) async-start(), calls=%async_computation.2 | async-start | bytes 393216 | tf_op jit(solution)/shard_map/psum | solution.py:127
  426.4 4.6 collective-permute-start.3
  428.4 7.5 collective-permute-start.2
  483.3 361.0 %all-reduce.11.cloned.1.call-start = ((), (), s32[]{:S(2)}) async-start(), calls=%async_computation.3 | async-start | bytes 393216 | tf_op jit(solution)/shard_map/psum | solution.py:127
  636.3 4.6 collective-permute-start.5
  638.2 7.5 collective-permute-start.4
  846.1 4.4 collective-permute-start.7
  848.0 7.5 collective-permute-start.6
Sparse Core Ops, SparseCore 0:
  56.7 158.1 all-reduce.4
  273.6 150.9 all-reduce.6
  483.4 151.0 all-reduce.8
  693.3 150.9 all-reduce.10
where the time goes:
time: 873 us; the launch traced here: 864 us
  waiting for transfers between devices  631 us (72%)
  local copies, waits for them, and re-layouts  127 us (15%)
  other arithmetic  64.5 us (7%)
  starting transfers between devices  18.1 us (2%)
  between operations  14.3 us (2%)
  matrix products  9.5 us (1%)
    psum x4, waiting for transfers between devices, body(): summed = lax.psum(partial_normals, 'bl')  611 us
    gather x4, local copies, waits for them, and re-layouts, local_normals(): left_gain = jnp.take(gain_now, leading_station, axis=3)[:, :, :, None, :]  41.8 us
    gather x4, local copies, waits for them, and re-layouts, local_normals(): right_gain = jnp.take(gain_now, second_station, axis=3)[:, :, :, None, :]  40.2 us
    select_n x4, other arithmetic, local_normals(): left_gain = jnp.take(gain_now, leading_station, axis=3)[:, :, :, None, :]  22.7 us
    select_n x4, other arithmetic, local_normals(): right_gain = jnp.take(gain_now, second_station, axis=3)[:, :, :, None, :]  22.7 us
    ppermute x4, waiting for transfers between devices, padded_2(): before = lax.ppermute(last, axis, up)  19.3 us
    mul x12, local copies, waits for them, and re-layouts, station_terms(): fwd_re = left_re * sky_re - left_im * sky_im  19.2 us
    mul x12, local copies, waits for them, and re-layouts, station_terms(): one_re = fwd_re * right_re + fwd_im * right_im  19.1 us
  transfers between devices with their start and end apart: 12, of which 9 were waited for; matrix products, arithmetic and copies ran while one was open for 0% of the time, Pallas kernels for 0%

commit v1 on v0

v1 whole, which is shorter than its diff:
```python
import functools

import jax
import jax.numpy as jnp
from jax import lax
from jax.experimental import pallas as pl
from jax.experimental.pallas import tpu as pltpu
from jax.sharding import PartitionSpec as P

ITERS = 4
DIRS = 6
CHANS = 4
TIMES = 2
STATIONS = 512
NZ, NX = 8, 4
LANE = 128
BLOCKS = STATIONS // LANE
MESH = pl.DeviceIdType.MESH
F32, BF16 = jnp.float32, jnp.bfloat16


def hops(kz, kx):
    return min(kz, NZ - kz) + min(kx, NX - kx)


STEPS = sorted(
    [(kz, kx) for kz in range(NZ) for kx in range(NX) if kz or kx], key=lambda k: -hops(*k)
)


def owner_of(z):
    return jnp.logical_and(z != 3, z != 7), jnp.minimum(jnp.where(z > 3, z - 1, z), DIRS - 1)


def wait_for(ref, sem):
    pltpu.make_async_copy(ref, ref, sem).wait()


def kernel(
    nf, rho, vis_ref, sky_ref, ids_ref, gains_ref, width_ref, out_ref,
    gbuf, glhs, gat, oht, oh, terms, snd, rbuf, halo, upd, wts,
    rs_send, rs_recv, ag_send, ag_recv, ex_send, ex_recv,
):
    blocal = ids_ref.shape[1]
    f, bl = lax.axis_index("freq"), lax.axis_index("bl")
    z, x = lax.div(bl, NX), lax.rem(bl, NX)
    own, mine = owner_of(z)
    not_own = jnp.logical_not(own)
    has_up, has_down = f < nf - 1, f > 0

    def peer(kz, kx):
        return lax.rem(z + kz, NZ), lax.rem(x + kx, NX)

    halo[...] = jnp.zeros_like(halo)

    barrier = pltpu.get_barrier_semaphore()
    for kz, kx in STEPS:
        tz, tx = peer(kz, kx)
        pl.semaphore_signal(barrier, inc=1, device_id=(f, tz * NX + tx), device_id_type=MESH)

    for step in (1, nf - 1):
        neighbour = lax.rem(f + step, nf)
        pl.semaphore_signal(barrier, inc=1, device_id=(neighbour, bl), device_id_type=MESH)

    sub = lax.broadcasted_iota(jnp.int32, (8, LANE), 0)
    top = sub < CHANS

    for d in range(DIRS):
        for b in range(BLOCKS):
            lanes = slice(b * LANE, (b + 1) * LANE)
            gbuf[d, b] = jnp.concatenate(
                [gains_ref[0, d, :, lanes], gains_ref[1, d, :, lanes]], axis=0
            )

    spread = jnp.full((8, LANE), width_ref[mine], jnp.int32).astype(F32)
    chan = jnp.bitwise_and(sub, CHANS - 1)
    taps = []
    for j in range(3 * CHANS):
        shift = j - CHANS - chan
        there = f * CHANS + (j - CHANS)
        inside = (jnp.abs(shift) <= CHANS) & (there >= 0) & (there < nf * CHANS)
        distance = shift.astype(F32)
        taps.append(
            jnp.where(inside, jnp.exp(-(distance * distance) / (2.0 * spread * spread)), 0.0)
        )
    total = functools.reduce(jnp.add, taps)
    for j in range(3 * CHANS):
        wts[j] = taps[j] / total

    def fill(i, _):
        for h in range(2):
            row = ids_ref[h : h + 1, pl.ds(pl.multiple_of(i * LANE, LANE), LANE)]
            at = pl.multiple_of(h * blocal + i * LANE, LANE)
            station = lax.broadcasted_iota(jnp.int32, (STATIONS, LANE), 0)
            oht[:, pl.ds(at, LANE)] = jnp.where(station == row, 1.0, 0.0).astype(BF16)
            column = jnp.transpose(jnp.broadcast_to(row, (LANE, LANE)))
            for b in range(BLOCKS):
                station = lax.broadcasted_iota(jnp.int32, (LANE, LANE), 1) + b * LANE
                oh[pl.ds(at, LANE), b * LANE : (b + 1) * LANE] = jnp.where(
                    station == column, 1.0, 0.0
                ).astype(BF16)
        return 0

    lax.fori_loop(0, blocal // LANE, fill, 0)

    pl.semaphore_wait(barrier, len(STEPS) + 2)

    def swap(tile):
        return pltpu.roll(tile, CHANS, 0)

    def parts_of(tile):
        other = swap(tile)
        return jnp.where(top, tile, other), jnp.where(top, other, tile)

    def fold(a, b):
        return jnp.where(top, a, b) + swap(jnp.where(top, b, a))

    def chunk(i, _):
        lanes = pl.ds(pl.multiple_of(i * LANE, LANE), LANE)
        after = pl.ds(pl.multiple_of(blocal + i * LANE, LANE), LANE)
        sum_re, sum_im = vis_ref[0, :, lanes], vis_ref[1, :, lanes]
        kept = []
        for d in range(DIRS):
            hi, lo = slice(8 * d, 8 * d + 8), slice(8 * (DIRS + d), 8 * (DIRS + d) + 8)
            l_re, l_im = parts_of(gat[hi, lanes] + gat[lo, lanes])
            r_re, r_im = parts_of(gat[hi, after] + gat[lo, after])
            m_re, m_im = sky_ref[2 * d, :, lanes], sky_ref[2 * d + 1, :, lanes]
            z_re = l_re * m_re - l_im * m_im
            z_im = l_re * m_im + l_im * m_re
            y_re = r_re * m_re + r_im * m_im
            y_im = r_re * m_im - r_im * m_re
            u_re = z_re * r_re + z_im * r_im
            u_im = z_im * r_re - z_re * r_im
            sum_re, sum_im = sum_re - u_re, sum_im - u_im
            kept.append((z_re, z_im, y_re, y_im, u_re, u_im))
        first, second, first_den, second_den = [], [], [], []
        for z_re, z_im, y_re, y_im, u_re, u_im in kept:
            res_re, res_im = sum_re + u_re, sum_im + u_im
            first.append(fold(res_re * y_re + res_im * y_im, res_im * y_re - res_re * y_im))
            second.append(fold(res_re * z_re + res_im * z_im, res_re * z_im - res_im * z_re))
            first_den.append(y_re * y_re + y_im * y_im)
            second_den.append(z_re * z_re + z_im * z_im)
        for d in range(0, DIRS, 2):
            first.append(fold(first_den[d], first_den[d + 1]))
            second.append(fold(second_den[d], second_den[d + 1]))
        pad = jnp.zeros((8, LANE), F32)
        terms[:, lanes] = jnp.concatenate([*first, pad], axis=0).astype(BF16)
        terms[:, after] = jnp.concatenate([*second, pad], axis=0).astype(BF16)
        return 0

    def row_of(ref, e):
        return jnp.where(
            top,
            jnp.broadcast_to(ref[e : e + 1, :], (8, LANE)),
            jnp.broadcast_to(ref[CHANS + e : CHANS + e + 1, :], (8, LANE)),
        )

    def smooth(ref, side):
        return functools.reduce(
            jnp.add, [wts[side * CHANS + e] * row_of(ref, e) for e in range(CHANS)]
        )

    def sweep(it, _):
        parity = lax.rem(it, 2)
        for b in range(BLOCKS):
            for d in range(0, DIRS, 2):
                value = jnp.concatenate([gbuf[d, b], gbuf[d + 1, b]], axis=0)
                high = value.astype(BF16)
                low = (value - high.astype(F32)).astype(BF16)
                lanes = slice(b * LANE, (b + 1) * LANE)
                glhs[8 * d : 8 * d + 16, lanes] = high
                glhs[8 * (DIRS + d) : 8 * (DIRS + d) + 16, lanes] = low
        gat[...] = jnp.dot(glhs[...], oht[...], preferred_element_type=F32)
        lax.fori_loop(0, blocal // LANE, chunk, 0)
        normals = jnp.dot(terms[...], oh[...], preferred_element_type=F32)
        for b in range(BLOCKS):
            lanes = slice(b * LANE, (b + 1) * LANE)
            for d in range(DIRS):
                snd[d, b, 0:8] = normals[8 * d : 8 * d + 8, lanes]
                den = 8 * DIRS + CHANS * d
                snd[d, b, 8:12] = normals[den : den + CHANS, lanes]

        for kz, kx in STEPS:
            tz, tx = peer(kz, kx)
            there, which = owner_of(tz)

            @pl.when(there)
            def _():
                pltpu.make_async_remote_copy(
                    src_ref=snd.at[which, tx, pl.ds(0, 12)],
                    dst_ref=rbuf.at[kz * NX + kx, pl.ds(0, 12)],
                    send_sem=rs_send,
                    recv_sem=rs_recv,
                    device_id=(f, tz * NX + tx),
                    device_id_type=MESH,
                ).start()

        @pl.when(own)
        def _():
            wait_for(rbuf.at[pl.ds(1, 31), pl.ds(0, 12)], rs_recv)
            num, den = snd[mine, x, 0:8], snd[mine, x, 8:12]
            for k in range(1, NZ * NX):
                num = num + rbuf[k, 0:8]
                den = den + rbuf[k, 8:12]
            den = jnp.concatenate([den, den], axis=0)
            now = gbuf[mine, x]
            upd[...] = 0.5 * (now + (num + rho * now) / (den + rho))

            @pl.when(has_up)
            def _():
                pltpu.make_async_remote_copy(
                    src_ref=upd, dst_ref=halo.at[parity, 0],
                    send_sem=ex_send.at[0], recv_sem=ex_recv.at[parity, 0],
                    device_id=(f + 1, bl), device_id_type=MESH,
                ).start()

            @pl.when(has_down)
            def _():
                pltpu.make_async_remote_copy(
                    src_ref=upd, dst_ref=halo.at[parity, 1],
                    send_sem=ex_send.at[1], recv_sem=ex_recv.at[parity, 1],
                    device_id=(f - 1, bl), device_id_type=MESH,
                ).start()

            inner = smooth(upd, 1)

            @pl.when(it > 0)
            def _():
                wait_for(rbuf.at[pl.ds(1, 31), pl.ds(0, 8)], ag_send)

            @pl.when(has_down)
            def _():
                wait_for(halo.at[parity, 0], ex_recv.at[parity, 0])

            @pl.when(has_up)
            def _():
                wait_for(halo.at[parity, 1], ex_recv.at[parity, 1])

            gbuf[mine, x] = inner + smooth(halo.at[parity, 0], 0) + smooth(halo.at[parity, 1], 2)
            for kz, kx in STEPS:
                tz, tx = peer(kz, kx)
                pltpu.make_async_remote_copy(
                    src_ref=gbuf.at[mine, x], dst_ref=gbuf.at[mine, x],
                    send_sem=ag_send, recv_sem=ag_recv,
                    device_id=(f, tz * NX + tx), device_id_type=MESH,
                ).start()
            wait_for(rbuf.at[pl.ds(0, 23), pl.ds(0, 8)], ag_recv)
            wait_for(rbuf.at[pl.ds(0, 23), pl.ds(0, 12)], rs_send)

            @pl.when(has_up)
            def _():
                wait_for(upd, ex_send.at[0])

            @pl.when(has_down)
            def _():
                wait_for(upd, ex_send.at[1])

        @pl.when(not_own)
        def _():
            wait_for(rbuf.at[pl.ds(0, 24), pl.ds(0, 8)], ag_recv)
            wait_for(rbuf.at[pl.ds(0, 24), pl.ds(0, 12)], rs_send)

        return 0

    lax.fori_loop(0, ITERS, sweep, 0)

    @pl.when(own)
    def _():
        wait_for(rbuf.at[pl.ds(1, 31), pl.ds(0, 8)], ag_send)

    out_ref[...] = gbuf[...]


def body(visibilities, predicted_sky, station_pairs, start_gains, kernel_width):
    chans, stations = start_gains.shape[2:]
    blocal = station_pairs.shape[1]
    nf = lax.axis_size("freq")
    rho = float(TIMES * blocal * lax.axis_size("bl") / stations)
    vis = jnp.swapaxes(visibilities, 1, 2).reshape(2, 8, blocal).astype(F32)
    sky = jnp.swapaxes(predicted_sky, 2, 3).reshape(2 * DIRS, 8, blocal).astype(F32)
    whole = pl.BlockSpec(memory_space=pltpu.VMEM)
    gains = pl.pallas_call(
        functools.partial(kernel, nf, rho),
        out_shape=jax.ShapeDtypeStruct((DIRS, BLOCKS, 8, LANE), F32),
        in_specs=[whole, whole, whole, whole, pl.BlockSpec(memory_space=pltpu.SMEM)],
        out_specs=whole,
        scratch_shapes=[
            pltpu.VMEM((DIRS, BLOCKS, 8, LANE), F32),
            pltpu.VMEM((16 * DIRS, STATIONS), BF16),
            pltpu.VMEM((16 * DIRS, 2 * blocal), F32),
            pltpu.VMEM((STATIONS, 2 * blocal), BF16),
            pltpu.VMEM((2 * blocal, STATIONS), BF16),
            pltpu.VMEM((80, 2 * blocal), BF16),
            pltpu.VMEM((DIRS, BLOCKS, 16, LANE), F32),
            pltpu.VMEM((NZ * NX, 16, LANE), F32),
            pltpu.VMEM((2, 2, 8, LANE), F32),
            pltpu.VMEM((8, LANE), F32),
            pltpu.VMEM((3 * CHANS, 8, LANE), F32),
            pltpu.SemaphoreType.DMA,
            pltpu.SemaphoreType.DMA,
            pltpu.SemaphoreType.DMA,
            pltpu.SemaphoreType.DMA,
            pltpu.SemaphoreType.DMA((2,)),
            pltpu.SemaphoreType.DMA((2, 2)),
        ],
        compiler_params=pltpu.CompilerParams(
            collective_id=0, has_side_effects=True, vmem_limit_bytes=48 * 1024 * 1024
        ),
    )(vis, sky, station_pairs, start_gains, kernel_width)
    gains = gains.reshape(DIRS, BLOCKS, 2, chans, LANE)
    return gains.transpose(2, 0, 3, 1, 4).reshape(2, DIRS, chans, stations)


def solution(mesh):
    in_specs = (
        P(None, "freq", None, "bl"),
        P(None, None, "freq", None, "bl"),
        P(None, "bl"),
        P(None, None, "freq", None),
        P(),
    )
    out_specs = P(None, None, "freq", None)
    return jax.shard_map(body, mesh=mesh, in_specs=in_specs, out_specs=out_specs, check_vma=False)
```

time: 873 us -> 85.7 us (0.10)
  the two profiles are of different devices: /device:TPU:32 before, /device:TPU:25 now
where the time goes in v1:
time: 85.7 us; the launch traced here: 85.5 us
  Pallas kernels  81.8 us (95%)
  local copies, waits for them, and re-layouts  2.52 us (3%)
  other arithmetic  1.1 us (1%)
    pallas_call x1, Pallas kernels, body(): pl.pallas_call(functools.partial(kernel, nf, rho), out_shape=jax.ShapeDty...  81.8 us

profile of v1, /device:TPU:25, one launch (start us, length us, event | category | flops | bytes accessed | tf_op | source)
XLA Modules:
  0.0 85.5 jit_solution(10557247602918238279)
XLA Ops:
  0.0 1.1 %convert_bitcast_fusion = f32[6,2,2,4,1024]{4,2,3,1,0:T(2,128)S(1)} fusion(bf16[6,2,4,2,1024]{4,3,2,1,0:T(2,128)(2,1)} %param.6), kind=kLoop, calls=%fused_computation | loop fusion | flops 98304 | bytes 589824 | tf_op jit(solution)/shard_map/convert_element_type | solution.py:280
  1.1 0.2 copy.7
  1.2 0.0 copy-start.3
  1.3 0.1 reshape.15.sky_ref
  1.4 0.6 copy-done.3
  2.1 0.0 copy-start
  2.1 0.0 copy-start.1
  2.1 0.0 copy-start.2
  2.1 0.8 copy-done
  3.0 0.0 copy-done.1
  3.0 0.0 copy-done.2
  3.0 81.8 %shard_map.55 = f32[6,4,8,128]{3,2,1,0:T(8,128)S(1)} custom-call(f32[2,8,1024]{2,1,0:T(8,128)S(1)} %reshape.14.vis_ref, f32[12,8,1024]{2,1,0:T(8,128)S(1)} %reshape.15.sky_ref, s32[2,1024]{1,0:T(2,128)S(1)} %copy-done.1, f32[2,6,4,512]{3,2,1,0:T(4,128)S(1)} %copy-done, s32[6]{0:T(128)S(1)} %copy-done.2), custom_call_target="tpu_custom_call" | custom-call | tf_op jit(solution)/shard_map/pallas_call | solution.py:282
  84.8 0.7 reshape.13
  (4 shorter events, 0.1 us)
Async XLA Ops:
  1.2 0.8 copy-start.3
  2.1 0.9 %copy-start = (f32[2,6,4,512]{3,2,1,0:T(4,128)S(1)}, f32[2,6,4,512]{3,2,1,0:T(4,128)}, u32[]{:S(2)}) copy-start(f32[2,6,4,512]{3,2,1,0:T(4,128)} %gains_ref.1) | copy-start | bytes 294916
  2.1 0.9 %copy-start.1 = (s32[2,1024]{1,0:T(2,128)S(1)}, s32[2,1024]{1,0:T(2,128)}, u32[]{:S(2)}) copy-start(s32[2,1024]{1,0:T(2,128)} %ids_ref.1) | copy-start | bytes 24580
  2.1 0.9 %copy-start.2 = (s32[6]{0:T(128)S(1)}, s32[6]{0:T(128)}, u32[]{:S(2)}) copy-start(s32[6]{0:T(128)} %width_ref.1) | copy-start | bytes 76

commit v2 on v1

v2 whole, which is shorter than its diff:
```python
import functools

import jax
import jax.numpy as jnp
from jax import lax
from jax.experimental import pallas as pl
from jax.experimental.pallas import tpu as pltpu
from jax.sharding import PartitionSpec as P

ITERS = 4
DIRS = 6
CHANS = 4
TIMES = 2
STATIONS = 512
NZ, NX = 8, 4
LANE = 128
BLOCKS = STATIONS // LANE
MESH = pl.DeviceIdType.MESH
F32, BF16 = jnp.float32, jnp.bfloat16


def hops(kz, kx):
    return min(kz, NZ - kz) + min(kx, NX - kx)


STEPS = sorted(
    [(kz, kx) for kz in range(NZ) for kx in range(NX) if kz or kx], key=lambda k: -hops(*k)
)
X_STEPS = sorted(range(NX), key=lambda kx: -hops(0, kx))


def owner_of(z):
    return jnp.logical_and(z != 3, z != 7), jnp.minimum(jnp.where(z > 3, z - 1, z), DIRS - 1)


def wait_for(ref, sem):
    pltpu.make_async_copy(ref, ref, sem).wait()


def kernel(
    nf, rho, vis_hbm, sky_hbm, ids_hbm, gains_hbm, width_hbm, out_ref,
    vis_raw, sky_raw, ids_ref, gains_ref, width_ref, vis_ref, sky_ref,
    gbuf, gat, oh, terms, snd, rbuf, halo, upd, wts,
    in_sems, rs_send, rs_recv, ag_send, ag_recv, ex_send, ex_recv,
):
    blocal = ids_ref.shape[1]
    f, bl = lax.axis_index("freq"), lax.axis_index("bl")
    z, x = lax.div(bl, NX), lax.rem(bl, NX)
    own, mine = owner_of(z)
    not_own = jnp.logical_not(own)
    has_up, has_down = f < nf - 1, f > 0

    def peer(kz, kx):
        return lax.rem(z + kz, NZ), lax.rem(x + kx, NX)

    halo[...] = jnp.zeros_like(halo)

    barrier = pltpu.get_barrier_semaphore()
    for kz, kx in STEPS:
        tz, tx = peer(kz, kx)
        pl.semaphore_signal(barrier, inc=1, device_id=(f, tz * NX + tx), device_id_type=MESH)
    for step in (1, nf - 1):
        neighbour = lax.rem(f + step, nf)
        pl.semaphore_signal(barrier, inc=1, device_id=(neighbour, bl), device_id_type=MESH)

    loads = [
        pltpu.make_async_copy(src, dst, in_sems.at[i])
        for i, (src, dst) in enumerate(
            [
                (ids_hbm, ids_ref),
                (width_hbm, width_ref),
                (gains_hbm, gains_ref),
                (vis_hbm, vis_raw),
                (sky_hbm, sky_raw),
            ]
        )
    ]
    for load in loads:
        load.start()

    sub = lax.broadcasted_iota(jnp.int32, (8, LANE), 0)
    top = sub < CHANS

    loads[0].wait()

    def fill(i, _):
        for h in range(2):
            row = ids_ref[h : h + 1, pl.ds(pl.multiple_of(i * LANE, LANE), LANE)]
            at = pl.multiple_of(h * blocal + i * LANE, LANE)
            column = jnp.transpose(jnp.broadcast_to(row, (LANE, LANE)))
            for b in range(BLOCKS):
                station = lax.broadcasted_iota(jnp.int32, (LANE, LANE), 1) + b * LANE
                oh[b, pl.ds(at, LANE)] = jnp.where(station == column, 1.0, 0.0).astype(BF16)
        return 0

    lax.fori_loop(0, blocal // LANE, fill, 0)

    loads[1].wait()
    spread = jnp.full((8, LANE), width_ref[mine], jnp.int32).astype(F32)
    chan = jnp.bitwise_and(sub, CHANS - 1)
    taps = []
    for j in range(3 * CHANS):
        shift = j - CHANS - chan
        there = f * CHANS + (j - CHANS)
        inside = (jnp.abs(shift) <= CHANS) & (there >= 0) & (there < nf * CHANS)
        distance = shift.astype(F32)
        taps.append(
            jnp.where(inside, jnp.exp(-(distance * distance) / (2.0 * spread * spread)), 0.0)
        )
    total = functools.reduce(jnp.add, taps)
    for j in range(3 * CHANS):
        wts[j] = taps[j] / total

    loads[2].wait()
    for d in range(DIRS):
        for b in range(BLOCKS):
            lanes = slice(b * LANE, (b + 1) * LANE)
            gbuf[d, b] = jnp.concatenate(
                [gains_ref[0, d, :, lanes], gains_ref[1, d, :, lanes]], axis=0
            )

    loads[3].wait()
    for r in range(2):
        for c in range(CHANS):
            value = vis_raw[r, c].astype(F32)
            for t in range(TIMES):
                vis_ref[r, CHANS * t + c : CHANS * t + c + 1] = value[t : t + 1]
    loads[4].wait()

    def unpack(d, _):
        for r in range(2):
            for c in range(CHANS):
                value = sky_raw[d, r, c].astype(F32)
                for t in range(TIMES):
                    sky_ref[2 * d + r, CHANS * t + c : CHANS * t + c + 1] = value[t : t + 1]
        return 0

    lax.fori_loop(0, DIRS, unpack, 0)

    def swap(tile):
        return pltpu.roll(tile, CHANS, 0)

    def parts_of(tile):
        other = swap(tile)
        return jnp.where(top, tile, other), jnp.where(top, other, tile)

    def fold(a, b):
        return jnp.where(top, a, b) + swap(jnp.where(top, b, a))

    def ends(j):
        found = []
        for h in range(2):
            row = jnp.broadcast_to(ids_ref[h : h + 1, j * LANE : (j + 1) * LANE], (8, LANE))
            found.append((lax.shift_right_logical(row, 7), jnp.bitwise_and(row, LANE - 1)))
        return found

    def taken(d, block, at, lane, other):
        got = jnp.take_along_axis(gbuf[d, block], lane, axis=1)
        return jnp.where(at == block, got, other)

    def gather(steps, start):
        blocks = [lax.rem(x + k, NX) for k in steps]
        for j in range(blocal // LANE):
            for h, (at, lane) in enumerate(ends(j)):
                lanes = slice(h * blocal + j * LANE, h * blocal + (j + 1) * LANE)
                for d in range(DIRS):
                    rows = slice(8 * d, 8 * d + 8)
                    value = jnp.zeros((8, LANE), F32) if start else gat[rows, lanes]
                    for block in blocks:
                        value = taken(d, block, at, lane, value)
                    gat[rows, lanes] = value

    def chunk(j, last):
        lanes = slice(j * LANE, (j + 1) * LANE)
        after = slice(blocal + j * LANE, blocal + (j + 1) * LANE)
        (p_at, p_lane), (q_at, q_lane) = ends(j)
        sum_re, sum_im = vis_ref[0, :, lanes], vis_ref[1, :, lanes]
        kept = []
        for d in range(DIRS):
            rows = slice(8 * d, 8 * d + 8)
            l_re, l_im = parts_of(taken(d, last, p_at, p_lane, gat[rows, lanes]))
            r_re, r_im = parts_of(taken(d, last, q_at, q_lane, gat[rows, after]))
            m_re, m_im = sky_ref[2 * d, :, lanes], sky_ref[2 * d + 1, :, lanes]
            z_re = l_re * m_re - l_im * m_im
            z_im = l_re * m_im + l_im * m_re
            y_re = r_re * m_re + r_im * m_im
            y_im = r_re * m_im - r_im * m_re
            u_re = z_re * r_re + z_im * r_im
            u_im = z_im * r_re - z_re * r_im
            sum_re, sum_im = sum_re - u_re, sum_im - u_im
            kept.append((z_re, z_im, y_re, y_im, u_re, u_im))
        first, second, first_den, second_den = [], [], [], []
        for z_re, z_im, y_re, y_im, u_re, u_im in kept:
            res_re, res_im = sum_re + u_re, sum_im + u_im
            first.append(fold(res_re * y_re + res_im * y_im, res_im * y_re - res_re * y_im))
            second.append(fold(res_re * z_re + res_im * z_im, res_re * z_im - res_im * z_re))
            first_den.append(y_re * y_re + y_im * y_im)
            second_den.append(z_re * z_re + z_im * z_im)
        for d in range(0, DIRS, 2):
            first.append(fold(first_den[d], first_den[d + 1]))
            second.append(fold(second_den[d], second_den[d + 1]))
        pad = jnp.zeros((8, LANE), F32)
        terms[:, lanes] = jnp.concatenate([*first, pad], axis=0).astype(BF16)
        terms[:, after] = jnp.concatenate([*second, pad], axis=0).astype(BF16)

    def row_of(ref, e):
        return jnp.where(
            top,
            jnp.broadcast_to(ref[e : e + 1, :], (8, LANE)),
            jnp.broadcast_to(ref[CHANS + e : CHANS + e + 1, :], (8, LANE)),
        )

    def smooth(ref, side):
        return functools.reduce(
            jnp.add, [wts[side * CHANS + e] * row_of(ref, e) for e in range(CHANS)]
        )

    def finish_sends():
        @pl.when(own)
        def _():
            wait_for(rbuf.at[pl.ds(0, 23), pl.ds(0, 12)], rs_send)
            wait_for(rbuf.at[pl.ds(1, 31), pl.ds(0, 8)], ag_send)

            @pl.when(has_up)
            def _():
                wait_for(upd, ex_send.at[0])

            @pl.when(has_down)
            def _():
                wait_for(upd, ex_send.at[1])

        @pl.when(not_own)
        def _():
            wait_for(rbuf.at[pl.ds(0, 24), pl.ds(0, 12)], rs_send)

    def arrived(step):
        tiles = rbuf.at[pl.ds(0, DIRS), pl.ds(0, 8)]
        if step:
            wait_for(tiles, ag_recv.at[step])
        else:

            @pl.when(own)
            def _():
                wait_for(rbuf.at[pl.ds(0, DIRS - 1), pl.ds(0, 8)], ag_recv.at[0])

            @pl.when(not_own)
            def _():
                wait_for(tiles, ag_recv.at[0])

    def sweep(it, _):
        parity = lax.rem(it, 2)
        groups = ((0,), (1, 3), (2,))
        for group in groups:

            @pl.when(it > 0)
            def _():
                for step in group:
                    arrived(step)

            if group != groups[-1]:
                gather(group, group == groups[0])

        @pl.when(it > 0)
        def _():
            finish_sends()

        last = lax.rem(x + 2, NX)
        for j in range(blocal // LANE):
            chunk(j, last)

        @pl.when(it == 0)
        def _():
            pl.semaphore_wait(barrier, len(STEPS) + 2)

        for kx in X_STEPS:
            tx = lax.rem(x + kx, NX)
            normals = jnp.dot(terms[...], oh[tx], preferred_element_type=F32)
            for d in range(DIRS):
                snd[d, tx, 0:8] = normals[8 * d : 8 * d + 8]
                den = 8 * DIRS + CHANS * d
                snd[d, tx, 8:12] = normals[den : den + CHANS]
            for kz in sorted(range(NZ), key=lambda k: -hops(k, 0)):
                if not (kz or kx):
                    continue
                tz = lax.rem(z + kz, NZ)
                there, which = owner_of(tz)

                @pl.when(there)
                def _():
                    pltpu.make_async_remote_copy(
                        src_ref=snd.at[which, tx, pl.ds(0, 12)],
                        dst_ref=rbuf.at[kz * NX + kx, pl.ds(0, 12)],
                        send_sem=rs_send,
                        recv_sem=rs_recv,
                        device_id=(f, tz * NX + tx),
                        device_id_type=MESH,
                    ).start()

        @pl.when(own)
        def _():
            wait_for(rbuf.at[pl.ds(1, 31), pl.ds(0, 12)], rs_recv)
            num, den = snd[mine, x, 0:8], snd[mine, x, 8:12]
            for k in range(1, NZ * NX):
                num = num + rbuf[k, 0:8]
                den = den + rbuf[k, 8:12]
            den = jnp.concatenate([den, den], axis=0)
            now = gbuf[mine, x]
            upd[...] = 0.5 * (now + (num + rho * now) / (den + rho))

            @pl.when(has_up)
            def _():
                pltpu.make_async_remote_copy(
                    src_ref=upd, dst_ref=halo.at[parity, 0],
                    send_sem=ex_send.at[0], recv_sem=ex_recv.at[parity, 0],
                    device_id=(f + 1, bl), device_id_type=MESH,
                ).start()

            @pl.when(has_down)
            def _():
                pltpu.make_async_remote_copy(
                    src_ref=upd, dst_ref=halo.at[parity, 1],
                    send_sem=ex_send.at[1], recv_sem=ex_recv.at[parity, 1],
                    device_id=(f - 1, bl), device_id_type=MESH,
                ).start()

            inner = smooth(upd, 1)

            @pl.when(has_down)
            def _():
                wait_for(halo.at[parity, 0], ex_recv.at[parity, 0])

            @pl.when(has_up)
            def _():
                wait_for(halo.at[parity, 1], ex_recv.at[parity, 1])

            gbuf[mine, x] = inner + smooth(halo.at[parity, 0], 0) + smooth(halo.at[parity, 1], 2)
            for kz, kx in STEPS:
                tz, tx = peer(kz, kx)
                pltpu.make_async_remote_copy(
                    src_ref=gbuf.at[mine, x], dst_ref=gbuf.at[mine, x],
                    send_sem=ag_send, recv_sem=ag_recv.at[(NX - kx) % NX],
                    device_id=(f, tz * NX + tx), device_id_type=MESH,
                ).start()
        return 0

    lax.fori_loop(0, ITERS, sweep, 0)
    for step in range(NX):
        arrived(step)
    finish_sends()
    out_ref[...] = gbuf[...]


def body(visibilities, predicted_sky, station_pairs, start_gains, kernel_width):
    chans, stations = start_gains.shape[2:]
    blocal = station_pairs.shape[1]
    nf = lax.axis_size("freq")
    rho = float(TIMES * blocal * lax.axis_size("bl") / stations)
    hbm = pl.BlockSpec(memory_space=pltpu.HBM)
    gains = pl.pallas_call(
        functools.partial(kernel, nf, rho),
        out_shape=jax.ShapeDtypeStruct((DIRS, BLOCKS, 8, LANE), F32),
        in_specs=[hbm] * 5,
        out_specs=pl.BlockSpec(memory_space=pltpu.VMEM),
        scratch_shapes=[
            pltpu.VMEM(visibilities.shape, BF16),
            pltpu.VMEM(predicted_sky.shape, BF16),
            pltpu.VMEM(station_pairs.shape, jnp.int32),
            pltpu.VMEM(start_gains.shape, F32),
            pltpu.SMEM(kernel_width.shape, jnp.int32),
            pltpu.VMEM((2, 8, blocal), F32),
            pltpu.VMEM((2 * DIRS, 8, blocal), F32),
            pltpu.VMEM((DIRS, BLOCKS, 8, LANE), F32),
            pltpu.VMEM((8 * DIRS, 2 * blocal), F32),
            pltpu.VMEM((BLOCKS, 2 * blocal, LANE), BF16),
            pltpu.VMEM((80, 2 * blocal), BF16),
            pltpu.VMEM((DIRS, BLOCKS, 16, LANE), F32),
            pltpu.VMEM((NZ * NX, 16, LANE), F32),
            pltpu.VMEM((2, 2, 8, LANE), F32),
            pltpu.VMEM((8, LANE), F32),
            pltpu.VMEM((3 * CHANS, 8, LANE), F32),
            pltpu.SemaphoreType.DMA((5,)),
            pltpu.SemaphoreType.DMA,
            pltpu.SemaphoreType.DMA,
            pltpu.SemaphoreType.DMA,
            pltpu.SemaphoreType.DMA((NX,)),
            pltpu.SemaphoreType.DMA((2,)),
            pltpu.SemaphoreType.DMA((2, 2)),
        ],
        compiler_params=pltpu.CompilerParams(
            collective_id=0, has_side_effects=True, vmem_limit_bytes=63 * 1024 * 1024
        ),
    )(visibilities, predicted_sky, station_pairs, start_gains, kernel_width)
    gains = gains.reshape(DIRS, BLOCKS, 2, chans, LANE)
    return gains.transpose(2, 0, 3, 1, 4).reshape(2, DIRS, chans, stations)


def solution(mesh):
    in_specs = (
        P(None, "freq", None, "bl"),
        P(None, None, "freq", None, "bl"),
        P(None, "bl"),
        P(None, None, "freq", None),
        P(),
    )
    out_specs = P(None, None, "freq", None)
    return jax.shard_map(body, mesh=mesh, in_specs=in_specs, out_specs=out_specs, check_vma=False)
```

time: 85.7 us -> 82.5 us (0.963)
  other arithmetic: 1.1 us -> 0 us
  Pallas kernels: 81.8 us -> 80.7 us
  local copies, waits for them, and re-layouts: 2.52 us -> 1.62 us
    unnamed x8 -> x0, local copies, waits for them, and re-layouts: 1.45 us -> none
    convert_element_type x2 -> x0, other arithmetic: 1.1 us -> none  [the longest x1 1.07 us: body(): jnp.swapaxes(predicted_sky, 2, 3).reshape(2 * DIRS, 8, blocal).astype(F32)]
    pallas_call x1, Pallas kernels: 81.8 us -> 80.7 us  [body(): pl.pallas_call(functools.partial(kernel, nf, rho), out_shape=jax.ShapeDty...]
    transpose x1, local copies, waits for them, and re-layouts: 0.03 us -> 0.92 us  [body(): return gains.transpose(2, 0, 3, 1, 4).reshape(2, DIRS, chans, stations)]
where the time goes in v2:
time: 82.5 us; the launch traced here: 82.4 us
  Pallas kernels  80.7 us (98%)
  local copies, waits for them, and re-layouts  1.62 us (2%)
    pallas_call x1, Pallas kernels, body(): pl.pallas_call(functools.partial(kernel, nf, rho), out_shape=jax.ShapeDty...  80.7 us

profile of v2, /device:TPU:25, one launch (start us, length us, event | category | flops | bytes accessed | tf_op | source)
XLA Modules:
  0.0 82.4 jit_solution(11494227518198653376)
XLA Ops:
  0.0 80.7 %shard_map.55 = f32[6,4,8,128]{3,2,1,0:T(8,128)} custom-call(bf16[2,4,2,1024]{3,2,1,0:T(2,128)(2,1)} %vis_hbm.1, bf16[6,2,4,2,1024]{4,3,2,1,0:T(2,128)(2,1)} %sky_hbm.1, s32[2,1024]{1,0:T(2,128)} %ids_hbm.1, f32[2,6,4,512]{3,2,1,0:T(4,128)} %gains_hbm.1, s32[6]{0:T(128)} %width_hbm.1), custom_call_target="tpu_custom_call" | custom-call | tf_op jit(solution)/shard_map/pallas_call | solution.py:359
  80.7 0.9 %copy.6 = f32[2,6,4,4,128]{4,3,2,1,0:T(4,128)S(1)} copy(f32[2,6,4,4,128]{4,2,0,3,1:T(4,128)} %bitcast.3) | data formatting | bytes 196608 | tf_op jit(solution)/shard_map/transpose | solution.py:394
  81.7 0.7 reshape.7

commit v3 on v2

--- a/solution.py
+++ b/solution.py
@@ -347,7 +347,11 @@
     for step in range(NX):
         arrived(step)
     finish_sends()
-    out_ref[...] = gbuf[...]
+    for d in range(DIRS):
+        for b in range(BLOCKS):
+            for part in range(2):
+                rows = slice(CHANS * part, CHANS * part + CHANS)
+                out_ref[part, d, :, b * LANE : (b + 1) * LANE] = gbuf[d, b, rows]
 
 
 def body(visibilities, predicted_sky, station_pairs, start_gains, kernel_width):
@@ -358,7 +362,7 @@
     hbm = pl.BlockSpec(memory_space=pltpu.HBM)
     gains = pl.pallas_call(
         functools.partial(kernel, nf, rho),
-        out_shape=jax.ShapeDtypeStruct((DIRS, BLOCKS, 8, LANE), F32),
+        out_shape=jax.ShapeDtypeStruct(start_gains.shape, F32),
         in_specs=[hbm] * 5,
         out_specs=pl.BlockSpec(memory_space=pltpu.VMEM),
         scratch_shapes=[
@@ -387,11 +391,10 @@
             pltpu.SemaphoreType.DMA((2, 2)),
         ],
         compiler_params=pltpu.CompilerParams(
-            collective_id=0, has_side_effects=True, vmem_limit_bytes=63 * 1024 * 1024
+            collective_id=0, has_side_effects=True, vmem_limit_bytes=40 * 1024 * 1024
         ),
-    )(visibilities, predicted_sky, station_pairs, start_gains, kernel_width)
-    gains = gains.reshape(DIRS, BLOCKS, 2, chans, LANE)
-    return gains.transpose(2, 0, 3, 1, 4).reshape(2, DIRS, chans, stations)
+    )(*[pltpu.with_memory_space_constraint(v, pltpu.HBM) for v in (visibilities, predicted_sky, station_pairs, start_gains, kernel_width)])
+    return gains
 
 
 def solution(mesh):

time: 82.5 us -> 80.9 us (0.981)
  local copies, waits for them, and re-layouts: 1.62 us -> 0.64 us
    transpose x1 -> x0, local copies, waits for them, and re-layouts: 0.92 us -> none  [body(): return gains.transpose(2, 0, 3, 1, 4).reshape(2, DIRS, chans, stations)]
where the time goes in v3:
time: 80.9 us; the launch traced here: 80.8 us
  Pallas kernels  80.1 us (99%)
    pallas_call x1, Pallas kernels, body(): pl.pallas_call(functools.partial(kernel, nf, rho), out_shape=jax.ShapeDty...  80.1 us

profile of v3, /device:TPU:25, one launch (start us, length us, event | category | flops | bytes accessed | tf_op | source)
XLA Modules:
  0.0 80.8 jit_solution(7729046771825318195)
XLA Ops:
  0.0 80.1 %shard_map.55 = f32[2,6,4,512]{3,2,1,0:T(4,128)S(1)} custom-call(bf16[2,4,2,1024]{3,2,1,0:T(2,128)(2,1)} %vis_hbm.1, bf16[6,2,4,2,1024]{4,3,2,1,0:T(2,128)(2,1)} %sky_hbm.1, s32[2,1024]{1,0:T(2,128)} %ids_hbm.1, f32[2,6,4,512]{3,2,1,0:T(4,128)} %gains_hbm.1, s32[6]{0:T(128)} %width_hbm.1), custom_call_target="tpu_custom_call" | custom-call | tf_op jit(solution)/shard_map/pallas_call | solution.py:363
  80.1 0.6 copy.7

commit v4 on v3

--- a/solution.py
+++ b/solution.py
@@ -26,11 +26,14 @@
 STEPS = sorted(
     [(kz, kx) for kz in range(NZ) for kx in range(NX) if kz or kx], key=lambda k: -hops(*k)
 )
-X_STEPS = sorted(range(NX), key=lambda kx: -hops(0, kx))
-
-
-def owner_of(z):
-    return jnp.logical_and(z != 3, z != 7), jnp.minimum(jnp.where(z > 3, z - 1, z), DIRS - 1)
+GROUPS = ((2,), (1, 3), (0,))
+ARRIVALS = ((0,), (1,), (3, 2))
+
+
+def owner_of(z, x):
+    idle = lax.rem(x + 3, NX)
+    rank = z - jnp.where(z > idle, 1, 0) - jnp.where(z > idle + NX, 1, 0)
+    return lax.rem(z, NX) != idle, jnp.minimum(rank, DIRS - 1)
 
 
 def wait_for(ref, sem):
@@ -46,7 +49,7 @@
     blocal = ids_ref.shape[1]
     f, bl = lax.axis_index("freq"), lax.axis_index("bl")
     z, x = lax.div(bl, NX), lax.rem(bl, NX)
-    own, mine = owner_of(z)
+    own, mine = owner_of(z, x)
     not_own = jnp.logical_not(own)
     has_up, has_down = f < nf - 1, f > 0
 
@@ -154,9 +157,11 @@
             found.append((lax.shift_right_logical(row, 7), jnp.bitwise_and(row, LANE - 1)))
         return found
 
-    def taken(d, block, at, lane, other):
-        got = jnp.take_along_axis(gbuf[d, block], lane, axis=1)
-        return jnp.where(at == block, got, other)
+    def taken(d, blocks, at, lane, value):
+        for block in blocks:
+            got = jnp.take_along_axis(gbuf[d, block], lane, axis=1)
+            value = got if value is None else jnp.where(at == block, got, value)
+        return value
 
     def gather(steps, start):
         blocks = [lax.rem(x + k, NX) for k in steps]
@@ -165,10 +170,9 @@
                 lanes = slice(h * blocal + j * LANE, h * blocal + (j + 1) * LANE)
                 for d in range(DIRS):
                     rows = slice(8 * d, 8 * d + 8)
-                    value = jnp.zeros((8, LANE), F32) if start else gat[rows, lanes]
-                    for block in blocks:
-                        value = taken(d, block, at, lane, value)
-                    gat[rows, lanes] = value
+                    gat[rows, lanes] = taken(
+                        d, blocks, at, lane, None if start else gat[rows, lanes]
+                    )
 
     def chunk(j, last):
         lanes = slice(j * LANE, (j + 1) * LANE)
@@ -249,41 +253,44 @@
 
     def sweep(it, _):
         parity = lax.rem(it, 2)
-        groups = ((0,), (1, 3), (2,))
-        for group in groups:
+        for group in ARRIVALS:
 
             @pl.when(it > 0)
             def _():
                 for step in group:
                     arrived(step)
 
-            if group != groups[-1]:
-                gather(group, group == groups[0])
+            if group != ARRIVALS[-1]:
+                gather(group, group == ARRIVALS[0])
 
         @pl.when(it > 0)
         def _():
             finish_sends()
 
-        last = lax.rem(x + 2, NX)
+        last = [lax.rem(x + k, NX) for k in ARRIVALS[-1]]
         for j in range(blocal // LANE):
             chunk(j, last)
 
-        @pl.when(it == 0)
-        def _():
-            pl.semaphore_wait(barrier, len(STEPS) + 2)
-
-        for kx in X_STEPS:
-            tx = lax.rem(x + kx, NX)
-            normals = jnp.dot(terms[...], oh[tx], preferred_element_type=F32)
-            for d in range(DIRS):
-                snd[d, tx, 0:8] = normals[8 * d : 8 * d + 8]
-                den = 8 * DIRS + CHANS * d
-                snd[d, tx, 8:12] = normals[den : den + CHANS]
-            for kz in sorted(range(NZ), key=lambda k: -hops(k, 0)):
-                if not (kz or kx):
-                    continue
-                tz = lax.rem(z + kz, NZ)
-                there, which = owner_of(tz)
+        for group in GROUPS:
+            for kx in group:
+                tx = lax.rem(x + kx, NX)
+                normals = jnp.dot(terms[...], oh[tx], preferred_element_type=F32)
+                for d in range(DIRS):
+                    snd[d, tx, 0:8] = normals[8 * d : 8 * d + 8]
+                    den = 8 * DIRS + CHANS * d
+                    snd[d, tx, 8:12] = normals[den : den + CHANS]
+            if group == GROUPS[0]:
+
+                @pl.when(it == 0)
+                def _():
+                    pl.semaphore_wait(barrier, len(STEPS) + 2)
+
+            for kz, kx in sorted(
+                [(kz, kx) for kz in range(NZ) for kx in group if kz or kx],
+                key=lambda k: -hops(*k),
+            ):
+                tz, tx = peer(kz, kx)
+                there, which = owner_of(tz, tx)
 
                 @pl.when(there)
                 def _():
@@ -334,7 +341,7 @@
                 wait_for(halo.at[parity, 1], ex_recv.at[parity, 1])
 
             gbuf[mine, x] = inner + smooth(halo.at[parity, 0], 0) + smooth(halo.at[parity, 1], 2)
-            for kz, kx in STEPS:
+            for kz, kx in sorted(STEPS, key=lambda k: (-hops(k[0], 0), -hops(0, k[1]))):
                 tz, tx = peer(kz, kx)
                 pltpu.make_async_remote_copy(
                     src_ref=gbuf.at[mine, x], dst_ref=gbuf.at[mine, x],

time: 80.9 us -> 75.3 us (0.931)
  Pallas kernels: 80.1 us -> 74.5 us
    pallas_call x1, Pallas kernels: 80.1 us -> 74.5 us  [body(): pl.pallas_call(functools.partial(kernel, nf, rho), out_shape=jax.ShapeDty...]
where the time goes in v4:
time: 75.3 us; the launch traced here: 75.2 us
  Pallas kernels  74.5 us (99%)
    pallas_call x1, Pallas kernels, body(): pl.pallas_call(functools.partial(kernel, nf, rho), out_shape=jax.ShapeDty...  74.5 us

profile of v4, /device:TPU:25, one launch (start us, length us, event | category | flops | bytes accessed | tf_op | source)
XLA Modules:
  0.0 75.2 jit_solution(10360490317217392736)
XLA Ops:
  0.0 74.5 %shard_map.55 = f32[2,6,4,512]{3,2,1,0:T(4,128)S(1)} custom-call(bf16[2,4,2,1024]{3,2,1,0:T(2,128)(2,1)} %vis_hbm.1, bf16[6,2,4,2,1024]{4,3,2,1,0:T(2,128)(2,1)} %sky_hbm.1, s32[2,1024]{1,0:T(2,128)} %ids_hbm.1, f32[2,6,4,512]{3,2,1,0:T(4,128)} %gains_hbm.1, s32[6]{0:T(128)} %width_hbm.1), custom_call_target="tpu_custom_call" | custom-call | tf_op jit(solution)/shard_map/pallas_call | solution.py:370
  74.5 0.6 copy.7

commit v5 on v4

--- a/solution.py
+++ b/solution.py
@@ -27,6 +27,7 @@
     [(kz, kx) for kz in range(NZ) for kx in range(NX) if kz or kx], key=lambda k: -hops(*k)
 )
 GROUPS = ((2,), (1, 3), (0,))
+SUMS = (1, 3, 0, 2)
 ARRIVALS = ((0,), (1,), (3, 2))
 
 
@@ -36,6 +37,15 @@
     return lax.rem(z, NX) != idle, jnp.minimum(rank, DIRS - 1)
 
 
+def tree(values):
+    while len(values) > 1:
+        values = [
+            values[i] + values[i + 1] if i + 1 < len(values) else values[i]
+            for i in range(0, len(values), 2)
+        ]
+    return values[0]
+
+
 def wait_for(ref, sem):
     pltpu.make_async_copy(ref, ref, sem).wait()
 
@@ -43,7 +53,7 @@
 def kernel(
     nf, rho, vis_hbm, sky_hbm, ids_hbm, gains_hbm, width_hbm, out_ref,
     vis_raw, sky_raw, ids_ref, gains_ref, width_ref, vis_ref, sky_ref,
-    gbuf, gat, oh, terms, snd, rbuf, halo, upd, wts,
+    gbuf, gat, oh, terms, snd, rbuf, slots, halo, upd, wts,
     in_sems, rs_send, rs_recv, ag_send, ag_recv, ex_send, ex_recv,
 ):
     blocal = ids_ref.shape[1]
@@ -222,8 +232,8 @@
     def finish_sends():
         @pl.when(own)
         def _():
-            wait_for(rbuf.at[pl.ds(0, 23), pl.ds(0, 12)], rs_send)
-            wait_for(rbuf.at[pl.ds(1, 31), pl.ds(0, 8)], ag_send)
+            wait_for(slots.at[pl.ds(0, 23), pl.ds(0, 12)], rs_send)
+            wait_for(slots.at[pl.ds(0, 31), pl.ds(0, 8)], ag_send)
 
             @pl.when(has_up)
             def _():
@@ -235,17 +245,17 @@
 
         @pl.when(not_own)
         def _():
-            wait_for(rbuf.at[pl.ds(0, 24), pl.ds(0, 12)], rs_send)
+            wait_for(slots.at[pl.ds(0, 24), pl.ds(0, 12)], rs_send)
 
     def arrived(step):
-        tiles = rbuf.at[pl.ds(0, DIRS), pl.ds(0, 8)]
+        tiles = slots.at[pl.ds(0, DIRS), pl.ds(0, 8)]
         if step:
             wait_for(tiles, ag_recv.at[step])
         else:
 
             @pl.when(own)
             def _():
-                wait_for(rbuf.at[pl.ds(0, DIRS - 1), pl.ds(0, 8)], ag_recv.at[0])
+                wait_for(slots.at[pl.ds(0, DIRS - 1), pl.ds(0, 8)], ag_recv.at[0])
 
             @pl.when(not_own)
             def _():
@@ -296,20 +306,22 @@
                 def _():
                     pltpu.make_async_remote_copy(
                         src_ref=snd.at[which, tx, pl.ds(0, 12)],
-                        dst_ref=rbuf.at[kz * NX + kx, pl.ds(0, 12)],
+                        dst_ref=rbuf.at[kx, kz, pl.ds(0, 12)],
                         send_sem=rs_send,
-                        recv_sem=rs_recv,
+                        recv_sem=rs_recv.at[kx],
                         device_id=(f, tz * NX + tx),
                         device_id_type=MESH,
                     ).start()
 
         @pl.when(own)
         def _():
-            wait_for(rbuf.at[pl.ds(1, 31), pl.ds(0, 12)], rs_recv)
-            num, den = snd[mine, x, 0:8], snd[mine, x, 8:12]
-            for k in range(1, NZ * NX):
-                num = num + rbuf[k, 0:8]
-                den = den + rbuf[k, 8:12]
+            num, den = [snd[mine, x, 0:8]], [snd[mine, x, 8:12]]
+            for kx in SUMS:
+                senders = range(0 if kx else 1, NZ)
+                wait_for(rbuf.at[kx, pl.ds(senders[0], len(senders)), pl.ds(0, 12)], rs_recv.at[kx])
+                num.append(tree([rbuf[kx, kz, 0:8] for kz in senders]))
+                den.append(tree([rbuf[kx, kz, 8:12] for kz in senders]))
+            num, den = tree(num), tree(den)
             den = jnp.concatenate([den, den], axis=0)
             now = gbuf[mine, x]
             upd[...] = 0.5 * (now + (num + rho * now) / (den + rho))
@@ -385,13 +397,14 @@
             pltpu.VMEM((BLOCKS, 2 * blocal, LANE), BF16),
             pltpu.VMEM((80, 2 * blocal), BF16),
             pltpu.VMEM((DIRS, BLOCKS, 16, LANE), F32),
+            pltpu.VMEM((NX, NZ, 16, LANE), F32),
             pltpu.VMEM((NZ * NX, 16, LANE), F32),
             pltpu.VMEM((2, 2, 8, LANE), F32),
             pltpu.VMEM((8, LANE), F32),
             pltpu.VMEM((3 * CHANS, 8, LANE), F32),
             pltpu.SemaphoreType.DMA((5,)),
             pltpu.SemaphoreType.DMA,
-            pltpu.SemaphoreType.DMA,
+            pltpu.SemaphoreType.DMA((NX,)),
             pltpu.SemaphoreType.DMA,
             pltpu.SemaphoreType.DMA((NX,)),
             pltpu.SemaphoreType.DMA((2,)),

time: 75.3 us -> 76.2 us (1.012)
  Pallas kernels: 74.5 us -> 75.4 us
    pallas_call x1, Pallas kernels: 74.5 us -> 75.4 us  [body(): pl.pallas_call(functools.partial(kernel, nf, rho), out_shape=jax.ShapeDty...]
where the time goes in v5:
time: 76.2 us; the launch traced here: 76.1 us
  Pallas kernels  75.4 us (99%)
    pallas_call x1, Pallas kernels, body(): pl.pallas_call(functools.partial(kernel, nf, rho), out_shape=jax.ShapeDty...  75.4 us

profile of v5, /device:TPU:25, one launch (start us, length us, event | category | flops | bytes accessed | tf_op | source)
XLA Modules:
  0.0 76.1 jit_solution(2264420896638624721)
XLA Ops:
  0.0 75.4 %shard_map.55 = f32[2,6,4,512]{3,2,1,0:T(4,128)S(1)} custom-call(bf16[2,4,2,1024]{3,2,1,0:T(2,128)(2,1)} %vis_hbm.1, bf16[6,2,4,2,1024]{4,3,2,1,0:T(2,128)(2,1)} %sky_hbm.1, s32[2,1024]{1,0:T(2,128)} %ids_hbm.1, f32[2,6,4,512]{3,2,1,0:T(4,128)} %gains_hbm.1, s32[6]{0:T(128)} %width_hbm.1), custom_call_target="tpu_custom_call" | custom-call | tf_op jit(solution)/shard_map/pallas_call | solution.py:382
  75.4 0.6 copy.7
